TPU v7x, 32 devices: a whole 2x2x4 slice. The times are simulated.
32 devices in a mesh: ens: 2 (over y), lon: 4 (over z), lat: 4 (over x, core).
Axes of the slice: x: 2, y: 2, z: 4, core: 2. Of those that a mesh axis runs over, the one named last changes fastest.
Arguments:
- tracers: float32 [8, 16, 2048], P('ens', 'lat', 'lon'), parts along dimension 0, may hold values from -6 to 6
- forcing: float32 [8, 16, 2048], P('ens', 'lat', 'lon'), parts along dimension 0, may hold values from -4 to 4
- diffusivity: float32 [16, 2048], P('lat', 'lon'), may hold values from 0.02 to 0.2
- ocean_mask: int32 [16, 2048], P('lat', 'lon'), may hold values 0 or 1
- weight_in: bfloat16 [32, 4, 3, 3], replicated, may hold values from -1 to 1
- weight_mid: bfloat16 [32, 32, 3, 3], replicated, may hold values from -0.375 to 0.375
- weight_out: bfloat16 [4, 32, 3, 3], replicated, may hold values from -0.375 to 0.375
- sensitivity: float32 [8, 16, 2048], P('ens', 'lat', 'lon'), parts along dimension 0, may hold values from -6 to 6
Outputs:
- final_tracers: float32 [8, 16, 2048], P('ens', 'lat', 'lon'), parts along dimension 0
- gradient_in: float32 [64, 4, 3, 3], P('ens'), parts along dimension 0
- gradient_mid: float32 [64, 32, 3, 3], P('ens'), parts along dimension 0
- gradient_out: float32 [8, 32, 3, 3], P('ens'), parts along dimension 0
There are 2 independent parts, one for each index of `ens`. A program takes and returns all parts, laid end to end along the dimension named above; an argument that names none is the same for every part. Nothing has to cross between parts.
All inputs are finite; a program needn't handle non-finite values. No bound on the sum of `ocean_mask` on one device may be relied on, other than what follows from the above.
Results may differ from a plain program's by a relative error of at most 0.0065.
Values may be sent and summed in bfloat16 or wider, within the bound.
A program may use at most 64 MiB of HBM per device.

v0:
```python
import functools
import math

import jax
import jax.numpy as jnp
import numpy as np
from jax import lax
from jax.experimental import pallas as pl
from jax.experimental.pallas import tpu as pltpu
from jax.sharding import PartitionSpec as P

GAIN = 0.5
MESH = pl.DeviceIdType.MESH
F32 = jnp.float32
BF16 = jnp.bfloat16
TILE = 128
WIDE = 256
HID = 32
DEEP = 3 * HID
GROUP = 4
OWN_ROWS = 16


def dot(a, b):
    return jnp.dot(a, b, preferred_element_type=F32)


def dot_nt(a, b):
    return lax.dot_general(a, b, (((1,), (1,)), ((), ())), preferred_element_type=F32)


def left_of(v):
    return pltpu.roll(v, 1, 1)


def right_of(v):
    return pltpu.roll(v, WIDE - 1, 1)


def spread_matrix():
    m = np.zeros((80, 64), np.float32)
    for r in range(4):
        for c in range(4):
            for k in range(3):
                m[k * 16 + r * 4 + c, k * 16 + c * 4 + r] = 1
            m[48 + r * 4 + c, 48 + r] = 1
            m[64 + r * 4 + c, 52 + r] = 1
    return m


def kernel(
    n_lat, n_lon, halo, scale,
    tr_ref, fo_ref, ka_ref, ma_ref, wi_ref, wm_ref, wo_ref, se_ref, sp_ref,
    final_ref, gin_ref, gmid_ref, gout_ref,
    pk, rbuf, st, fo, se, ka, ma, lap, sixteen,
    t_if, t_ib, t_mf, t_mb, t_of, t_ob, t_tmp, t_wide,
    src, cc, h1, h2, l2, l1, acc, chunk, rs, total, fsrc, fdst,
    x_send, x_recv, f_send, f_recv, rs_send, rs_recv, ag_send, ag_recv,
):
    lat = lax.axis_index("lat")
    lon = lax.axis_index("lon")
    group = lat // GROUP
    j = lat % GROUP
    n_groups = n_lat // GROUP
    blocks = GROUP + 2 * halo
    rows = 4 * blocks
    reduce_here = n_lat * n_lon == 16

    barrier = pltpu.get_barrier_semaphore()
    if reduce_here:
        peers = [(dl, dz) for dz in range(n_lon) for dl in range(n_lat) if (dl, dz) != (0, 0)]
        peer_ids = [((lat + dl) % n_lat, (lon + dz) % n_lon) for dl, dz in peers]
    else:
        peer_ids = []
        for dg in (-1, 0, 1):
            for dj in range(GROUP):
                for dz in (-1, 0, 1):
                    if (dg, dj, dz) != (0, 0, 0):
                        other = (group + dg + n_groups) % n_groups
                        peer_ids.append((other * GROUP + (j + dj) % GROUP, (lon + dz + n_lon) % n_lon))
    for pl_lat, pl_lon in peer_ids:
        pl.semaphore_signal(
            barrier, inc=1, device_id={"lat": pl_lat, "lon": pl_lon}, device_id_type=MESH
        )

    pieces = [tr_ref[c] for c in range(4)] + [fo_ref[c] for c in range(4)] + [se_ref[c] for c in range(4)]
    pieces += [ka_ref[...], ma_ref[...].astype(F32)]
    for i, piece in enumerate(pieces):
        t_wide[i * 4 : i * 4 + 4, :] = piece
    t_wide[56:64, :] = jnp.zeros((8, 512), F32)
    packed = t_wide[...].astype(BF16)
    for t in range(GROUP):
        pk[t] = packed[:, t * TILE : (t + 1) * TILE]

    pl.semaphore_wait(barrier, len(peer_ids))

    waits = []

    def send(tile, slot, which, sem, to_lat, to_lon, when):
        copy = pltpu.make_async_remote_copy(
            src_ref=pk.at[tile],
            dst_ref=rbuf.at[slot, which],
            send_sem=x_send.at[sem],
            recv_sem=x_recv.at[slot, which],
            device_id={"lat": to_lat, "lon": to_lon},
            device_id_type=MESH,
        )
        if when is None:
            copy.start()
        else:
            pl.when(when)(copy.start)
        waits.append((copy, when))

    def keep(tile, slot, which, when):
        copy = pltpu.make_async_copy(pk.at[tile], rbuf.at[slot, which], x_recv.at[slot, which])
        if when is None:
            copy.start()
        else:
            pl.when(when)(copy.start)

    number = 0
    for dg in (0,) if halo == 0 else (-1, 0, 1):
        gate = None if dg == 0 else (j >= 1 if dg == 1 else j <= 2)
        to_group = ((group + dg + n_groups) % n_groups) * GROUP
        slot = j - 4 * dg + halo
        for s in (1, 2, 3, 0):
            t = (j + s) % GROUP
            own = dg == 0
            if own and s == 0:
                keep(t, slot, 1, None)
            else:
                send(t, slot, 1, number, to_group + t, lon, gate)
            number += 1
            if own and s == 3:
                keep(t, slot, 0, t != 3)
                when = t == 3
            else:
                when = gate
            send(
                t, slot, 0, number, to_group + (t + 1) % GROUP,
                (lon + (t == 3).astype(jnp.int32)) % n_lon, when,
            )
            number += 1
            if own and s == 1:
                keep(t, slot, 2, t != 0)
                when = t == 0
            else:
                when = gate
            send(
                t, slot, 2, number, to_group + (t + 3) % GROUP,
                (lon + n_lon - (t == 0).astype(jnp.int32)) % n_lon, when,
            )
            number += 1

    def banded_wide(parts, out_rows, target):
        t_tmp[...] = jnp.zeros_like(t_tmp)
        strip = jnp.concatenate(parts, axis=1)
        for r in range(4):
            t_tmp[r * out_rows : (r + 1) * out_rows, r * DEEP : r * DEEP + 3 * DEEP] = strip
        target[...] = t_tmp[0 : 4 * out_rows, 0 : 6 * DEEP].astype(BF16)

    def banded_narrow(parts, target):
        t_tmp[0:128, 0:128] = jnp.zeros((128, 128), F32)
        for r in range(4):
            for a in range(3):
                for b in range(3):
                    top = (r + a) * 16 + b * 4
                    t_tmp[top : top + 4, r * HID : (r + 1) * HID] = parts[a * 3 + b]
        target[...] = jnp.transpose(t_tmp[0:128, 0:128])[:, 0:96].astype(BF16)

    wi = [wi_ref[k].astype(F32) for k in range(9)]
    wm = [wm_ref[k].astype(F32) for k in range(9)]
    wo = [wo_ref[k].astype(F32) for k in range(9)]
    banded_narrow(wi, t_if)
    banded_wide(wm, HID, t_mf)
    banded_wide(wo, 4, t_of)
    banded_narrow(wo[::-1], t_ob)
    banded_wide([jnp.transpose(w) for w in wm[::-1]], HID, t_mb)
    banded_wide(wi[::-1], 4, t_ib)

    for buf in (h1, h2, l2, l1):
        for n in range(2):
            buf[n, 0:DEEP, :] = jnp.zeros((DEEP, WIDE), BF16)
            buf[n, (rows + 1) * DEEP : (rows + 2) * DEEP, :] = jnp.zeros((DEEP, WIDE), BF16)
    for buf in (src, cc):
        for n in range(2):
            buf[n, 0:16, :] = jnp.zeros((16, WIDE), BF16)
            buf[n, (rows + 1) * 16 : (rows + 2) * 16, :] = jnp.zeros((16, WIDE), BF16)
    sixteen[...] = jnp.zeros_like(sixteen)
    lap[...] = jnp.zeros_like(lap)

    def inside(per_row, count, first):
        if halo == 0:
            return None
        at = lax.broadcasted_iota(jnp.int32, (count, WIDE), 0) // per_row + first
        at = at + (group * GROUP - halo) * 4
        return ((at >= 0) & (at < n_lat * 4)).astype(F32)

    def clear(v, per_row, first):
        if halo == 0:
            return v
        return v * inside(per_row, v.shape[0], first)

    lane = lax.broadcasted_iota(jnp.int32, (80, TILE), 1)
    for w in range(blocks):
        for which in range(3):
            pltpu.make_async_copy(pk.at[0], rbuf.at[w, which], x_recv.at[w, which]).wait()
    for w in range(blocks):
        three = jnp.concatenate([rbuf[w, 1], rbuf[w, 0], rbuf[w, 2]], axis=1)
        got = dot(sp_ref[...], three)
        side = jnp.where(lane < TILE // 2, got[:, 2 * TILE :], got[:, TILE : 2 * TILE])
        both = jnp.concatenate([got[:, 0:TILE], side], axis=1)
        here = slice(w * 16, (w + 1) * 16)
        st[here, :] = clear(both[0:16], 4, 4 * w)
        fo[here, :] = both[16:32]
        se[here, :] = both[32:48]
        ka[here, :] = both[48:64]
        ma[here, :] = clear(both[64:80], 4, 4 * w)

    def put_narrow(target, n, v):
        for b, moved in enumerate((left_of(v), v, right_of(v))):
            for r in range(rows):
                sixteen[r * 16 + b * 4 : r * 16 + b * 4 + 4, :] = moved[r * 4 : r * 4 + 4]
        target[n, 16 : 16 + rows * 16, :] = sixteen[...].astype(BF16)

    def put_wide(target, n, w, v):
        v = clear(v, HID, 4 * w)
        for b, moved in enumerate((left_of(v), v, right_of(v))):
            moved = moved.astype(BF16)
            for r in range(4):
                top = (4 * w + r + 1) * DEEP + b * HID
                target[n, top : top + HID, :] = moved[r * HID : (r + 1) * HID]

    def centre(target, n, w):
        parts = []
        for r in range(4):
            top = (4 * w + r + 1) * DEEP + HID
            parts.append(target[n, top : top + HID, :])
        return jnp.concatenate(parts, axis=0).astype(F32)

    def narrow_window(target, n, w):
        return target[n, w * 64 : w * 64 + 96, :]

    def wide_window(target, n, w):
        return target[n, 4 * w * DEEP : 4 * w * DEEP + 6 * DEEP, :]

    def laplace(v):
        lap[8 : 8 + rows * 4, :] = v
        up = lap[4 : 4 + rows * 4, :]
        down = lap[12 : 12 + rows * 4, :]
        return up + down + left_of(v) + right_of(v) - 4.0 * v

    def forward(n, state):
        put_narrow(src, n, state)
        for w in range(blocks):
            put_wide(h1, n, w, jnp.tanh(dot(t_if[...], narrow_window(src, n, w))))
        for w in range(blocks):
            put_wide(h2, n, w, jnp.tanh(dot(t_mf[...], wide_window(h1, n, w))))
        closure = jnp.concatenate(
            [dot(t_of[...], wide_window(h2, n, w)) for w in range(blocks)], axis=0
        )
        return ma[...] * (state + ka[...] * laplace(state) + GAIN * closure + fo[...])

    def strip_wide(target, n):
        parts = []
        for s in range(OWN_ROWS + 2):
            top = (4 * halo + s) * DEEP
            parts.append(target[n, top : top + DEEP, 0:TILE])
        return jnp.concatenate(parts, axis=1)

    def strip_narrow(target, n):
        parts = []
        for s in range(OWN_ROWS + 2):
            top = (4 * halo + s) * 16
            parts.append(target[n, top : top + 16, 0:TILE])
        return jnp.concatenate(parts, axis=1)

    def strip_shifted(read, height):
        zero = jnp.zeros((height, TILE), BF16)
        cells = [read(r) for r in range(OWN_ROWS)]
        return jnp.concatenate(
            [jnp.concatenate([zero] * a + cells + [zero] * (2 - a), axis=1) for a in range(3)],
            axis=0,
        )

    def read_wide(target, n):
        def read(r):
            top = (4 * halo + r + 1) * DEEP + HID
            return target[n, top : top + HID, 0:TILE]

        return read

    def read_narrow(target, n):
        def read(r):
            top = (4 * halo + r + 1) * 16
            return target[n, top : top + 16, 0:TILE]

        return read

    def backward(n, masked, need_state):
        put_narrow(cc, n, GAIN * masked)
        grad_out = dot_nt(strip_shifted(read_narrow(cc, n), 16), strip_wide(h2, n))
        for w in range(blocks):
            slope = 1.0 - jnp.square(centre(h2, n, w))
            put_wide(l2, n, w, dot(t_ob[...], narrow_window(cc, n, w)) * slope)
        grad_mid = dot_nt(strip_shifted(read_wide(l2, n), HID), strip_wide(h1, n))
        for w in range(blocks):
            slope = 1.0 - jnp.square(centre(h1, n, w))
            put_wide(l1, n, w, dot(t_mb[...], wide_window(l2, n, w)) * slope)
        grad_in = dot_nt(strip_narrow(src, n), strip_shifted(read_wide(l1, n), HID))
        earlier = None
        if need_state:
            through = jnp.concatenate(
                [dot(t_ib[...], wide_window(l1, n, w)) for w in range(blocks)], axis=0
            )
            earlier = masked + laplace(ka[...] * masked) + through
        return earlier, (grad_in, grad_mid, grad_out)

    state = forward(0, st[...])
    final = forward(1, state)
    for i in range(GROUP):
        top = (halo + i) * 16
        fsrc[i] = final[top : top + 16, 0:TILE]
    for s in (1, 2, 3):
        i = (j + s) % GROUP
        copy = pltpu.make_async_remote_copy(
            src_ref=fsrc.at[i],
            dst_ref=fdst.at[j],
            send_sem=f_send.at[s],
            recv_sem=f_recv.at[j],
            device_id={"lat": group * GROUP + i, "lon": lon},
            device_id_type=MESH,
        )
        copy.start()
        waits.append((copy, None))
    pltpu.make_async_copy(fsrc.at[j], fdst.at[j], f_recv.at[j]).start()

    adjoint, late = backward(1, ma[...] * se[...], True)
    _, early = backward(0, ma[...] * adjoint, False)

    g_in, g_mid, g_out = (a + b for a, b in zip(late, early))
    acc[...] = jnp.zeros_like(acc)
    acc[0:96, 0:96] = g_mid * scale
    for a in range(3):
        acc[96 + a * 4 : 100 + a * 4, 0:96] = g_out[a * 16 + 4 : a * 16 + 8] * scale
    acc[108:120, 0:96] = g_in[0:12] * scale

    if reduce_here:
        rank = lon * n_lat + lat
        sums = []
        for o, (to_lat, to_lon) in enumerate(peer_ids):
            other = to_lon * n_lat + to_lat
            copy = pltpu.make_async_remote_copy(
                src_ref=acc.at[pl.ds(pl.multiple_of(other * 8, 8), 8)],
                dst_ref=rs.at[o],
                send_sem=rs_send.at[o],
                recv_sem=rs_recv.at[o],
                device_id={"lat": to_lat, "lon": to_lon},
                device_id_type=MESH,
            )
            copy.start()
            waits.append((copy, None))
            sums.append(copy)
        mine = pl.ds(pl.multiple_of(rank * 8, 8), 8)
        whole = acc[mine, :]
        for o, copy in enumerate(sums):
            copy.wait_recv()
            whole = whole + rs[o]
        chunk[...] = whole
        total[mine, :] = whole
        gathered = []
        for o, (to_lat, to_lon) in enumerate(peer_ids):
            copy = pltpu.make_async_remote_copy(
                src_ref=chunk,
                dst_ref=total.at[mine],
                send_sem=ag_send.at[o],
                recv_sem=ag_recv.at[o],
                device_id={"lat": to_lat, "lon": to_lon},
                device_id_type=MESH,
            )
            copy.start()
            waits.append((copy, None))
            gathered.append(copy)

    for i in range(GROUP):
        pltpu.make_async_copy(fsrc.at[0], fdst.at[i], f_recv.at[i]).wait()
    for i in range(GROUP):
        for r in range(4):
            final_ref[r, :, i * TILE : (i + 1) * TILE] = fdst[i, r * 4 : r * 4 + 4, :]

    if reduce_here:
        for copy in gathered:
            copy.wait_recv()
        result = total[...]
    else:
        result = acc[...]
    for a in range(3):
        for b in range(3):
            k = a * 3 + b
            side = slice(b * HID, (b + 1) * HID)
            gmid_ref[k] = result[a * HID : (a + 1) * HID, side]
            gout_ref[k] = result[96 + a * 4 : 100 + a * 4, side]
            gin_ref[k] = result[108 + b * 4 : 112 + b * 4, a * HID : (a + 1) * HID]

    for copy, when in waits:
        if when is None:
            copy.wait_send()
        else:
            pl.when(when)(copy.wait_send)


def on_device(
    n_lat, n_lon,
    tracers, forcing, diffusivity, ocean_mask, weight_in, weight_mid, weight_out, sensitivity,
):
    halo = 0 if n_lat == GROUP else 3
    blocks = GROUP + 2 * halo
    rows = 4 * blocks
    scale = 1.0 / math.sqrt(tracers.shape[1] * n_lat * tracers.shape[2] * n_lon)
    vmem = pl.BlockSpec(memory_space=pltpu.VMEM)
    sends = 12 if halo == 0 else 36
    wi = weight_in.transpose(2, 3, 1, 0).reshape(9, 4, HID)
    wm = weight_mid.transpose(2, 3, 0, 1).reshape(9, HID, HID)
    wo = weight_out.transpose(2, 3, 0, 1).reshape(9, 4, HID)
    field = pltpu.VMEM((rows * 4, WIDE), F32)
    wide = pltpu.VMEM((2, (rows + 2) * DEEP, WIDE), BF16)
    narrow = pltpu.VMEM((2, (rows + 2) * 16, WIDE), BF16)
    final, g_in, g_mid, g_out = pl.pallas_call(
        functools.partial(kernel, n_lat, n_lon, halo, scale),
        out_shape=(
            jax.ShapeDtypeStruct((4, 4, 512), F32),
            jax.ShapeDtypeStruct((9, 4, HID), F32),
            jax.ShapeDtypeStruct((9, HID, HID), F32),
            jax.ShapeDtypeStruct((9, 4, HID), F32),
        ),
        in_specs=[vmem] * 9,
        out_specs=(vmem,) * 4,
        scratch_shapes=[
            pltpu.VMEM((GROUP, 64, TILE), BF16),
            pltpu.VMEM((blocks, 3, 64, TILE), BF16),
            field, field, field, field, field,
            pltpu.VMEM((rows * 4 + 16, WIDE), F32),
            pltpu.VMEM((rows * 16, WIDE), F32),
            pltpu.VMEM((128, 96), BF16),
            pltpu.VMEM((16, 576), BF16),
            pltpu.VMEM((128, 576), BF16),
            pltpu.VMEM((128, 576), BF16),
            pltpu.VMEM((16, 576), BF16),
            pltpu.VMEM((128, 96), BF16),
            pltpu.VMEM((128, 640), F32),
            pltpu.VMEM((64, 512), F32),
            narrow, narrow, wide, wide, wide, wide,
            pltpu.VMEM((128, 128), F32),
            pltpu.VMEM((8, 128), F32),
            pltpu.VMEM((15, 8, 128), F32),
            pltpu.VMEM((128, 128), F32),
            pltpu.VMEM((GROUP, 16, TILE), F32),
            pltpu.VMEM((GROUP, 16, TILE), F32),
            pltpu.SemaphoreType.DMA((sends,)),
            pltpu.SemaphoreType.DMA((blocks, 3)),
            pltpu.SemaphoreType.DMA((GROUP,)),
            pltpu.SemaphoreType.DMA((GROUP,)),
            pltpu.SemaphoreType.DMA((15,)),
            pltpu.SemaphoreType.DMA((15,)),
            pltpu.SemaphoreType.DMA((15,)),
            pltpu.SemaphoreType.DMA((15,)),
        ],
        compiler_params=pltpu.CompilerParams(
            collective_id=0, has_side_effects=True, vmem_limit_bytes=48 * 1024 * 1024
        ),
    )(
        tracers, forcing, diffusivity, ocean_mask, wi, wm, wo, sensitivity,
        jnp.asarray(spread_matrix(), BF16),
    )
    if n_lat * n_lon != 16:
        g_in, g_mid, g_out = lax.psum((g_in, g_mid, g_out), ("lon", "lat"))
    return (
        final.transpose(1, 0, 2),
        g_in.reshape(3, 3, 4, HID).transpose(3, 2, 0, 1),
        g_mid.reshape(3, 3, HID, HID).transpose(2, 3, 0, 1),
        g_out.reshape(3, 3, 4, HID).transpose(2, 3, 0, 1),
    )


def solution(mesh):
    field = P("ens", "lat", "lon")
    cells = P("lat", "lon")
    gradient = P("ens", None, None, None)
    return jax.shard_map(
        functools.partial(on_device, mesh.shape["lat"], mesh.shape["lon"]),
        mesh=mesh,
        in_specs=(field, field, cells, cells, P(), P(), P(), field),
        out_specs=(field, gradient, gradient, gradient),
        check_vma=False,
    )
```

profile of v0, /device:TPU:0, one launch (start us, length us, event | category | flops | bytes accessed | tf_op | source)
XLA Modules:
  0.0 33.4 jit_solution(3521419608234615116)
XLA Ops:
  0.6 0.0 copy-start
  0.6 0.9 %copy-done = bf16[32,32,3,3]{1,0,3,2:T(8,128)(2,1)S(1)} copy-done((bf16[32,32,3,3]{1,0,3,2:T(8,128)(2,1)S(1)}, bf16[32,32,3,3]{1,0,3,2:T(8,128)(2,1)}, u32[]{:S(2)}) %copy-start) | copy-done | bytes 18456
  1.5 0.0 copy-start.1
  1.5 0.8 %copy-done.1 = f32[4,4,512]{2,1,0:T(4,128)S(1)} copy-done((f32[4,4,512]{2,1,0:T(4,128)S(1)}, f32[4,4,512]{2,1,0:T(4,128)}, u32[]{:S(2)}) %copy-start.1) | copy-done | bytes 32792
  2.3 0.0 copy-start.2
  2.3 0.8 %copy-done.2 = f32[4,4,512]{2,1,0:T(4,128)S(1)} copy-done((f32[4,4,512]{2,1,0:T(4,128)S(1)}, f32[4,4,512]{2,1,0:T(4,128)}, u32[]{:S(2)}) %copy-start.2) | copy-done | bytes 32792
  3.0 0.0 copy-start.3
  3.0 0.8 %copy-done.3 = f32[4,4,512]{2,1,0:T(4,128)S(1)} copy-done((f32[4,4,512]{2,1,0:T(4,128)S(1)}, f32[4,4,512]{2,1,0:T(4,128)}, u32[]{:S(2)}) %copy-start.3) | copy-done | bytes 32792
  3.8 0.0 copy-start.4
  3.8 0.7 %copy-done.4 = bf16[80,64]{1,0:T(8,128)(2,1)S(1)} copy-done((bf16[80,64]{1,0:T(8,128)(2,1)S(1)}, bf16[80,64]{1,0:T(8,128)(2,1)}, u32[]{:S(2)}) %copy-start.4) | copy-done | bytes 10264
  4.5 0.0 copy-start.5
  4.5 0.7 %copy-done.5 = bf16[32,4,3,3]{0,1,3,2:T(4,128)(2,1)S(1)} copy-done((bf16[32,4,3,3]{0,1,3,2:T(4,128)(2,1)S(1)}, bf16[32,4,3,3]{0,1,3,2:T(4,128)(2,1)}, u32[]{:S(2)}) %copy-start.5) | copy-done | bytes 2328
  5.2 0.0 copy-start.6
  5.2 0.7 %copy-done.6 = bf16[4,32,3,3]{1,0,3,2:T(4,128)(2,1)S(1)} copy-done((bf16[4,32,3,3]{1,0,3,2:T(4,128)(2,1)S(1)}, bf16[4,32,3,3]{1,0,3,2:T(4,128)(2,1)}, u32[]{:S(2)}) %copy-start.6) | copy-done | bytes 2328
  5.9 0.0 copy-start.7
  5.9 0.7 %copy-done.7 = f32[4,512]{1,0:T(4,128)S(1)} copy-done((f32[4,512]{1,0:T(4,128)S(1)}, f32[4,512]{1,0:T(4,128)}, u32[]{:S(2)}) %copy-start.7) | copy-done | bytes 8216
  6.6 0.0 copy-start.8
  6.6 0.7 %copy-done.8 = s32[4,512]{1,0:T(4,128)S(1)} copy-done((s32[4,512]{1,0:T(4,128)S(1)}, s32[4,512]{1,0:T(4,128)}, u32[]{:S(2)}) %copy-start.8) | copy-done | bytes 8216
  7.3 23.5 %shard_map.120 = (f32[4,4,512]{2,1,0:T(4,128)S(1)}, f32[9,4,32]{2,1,0:T(4,128)S(1)}, f32[9,32,32]{2,1,0:T(8,128)S(1)}, f32[9,4,32]{2,1,0:T(4,128)S(1)}) custom-call(f32[4,4,512]{2,1,0:T(4,128)S(1)} %copy-done.1, f32[4,4,512]{2,1,0:T(4,128)S(1)} %copy-done.2, f32[4,512]{1,0:T(4,128)S(1)} %copy-done.7, s32[4,512]{1,0:T(4,128)S(1)} %copy-done.8, ...), custom_call_target="tpu_custom_call" | custom-call | tf_op jit(solution)/shard_map/pallas_call | solution.py:428
  30.9 0.6 %copy.13 = f32[4,4,512]{2,1,0:T(4,128)} copy(f32[4,4,512]{2,0,1:T(4,128)S(1)} %bitcast.21) | data formatting | bytes 65536
  31.5 0.6 %copy.17 = f32[32,4,3,3]{0,1,3,2:T(4,128)} copy(f32[32,4,3,3]{0,1,3,2:T(4,128)S(1)} %bitcast.23) | data formatting | bytes 9216
  32.1 0.7 %copy.18 = f32[32,32,3,3]{1,0,3,2:T(8,128)} copy(f32[32,32,3,3]{1,0,3,2:T(8,128)S(1)} %bitcast.19) | data formatting | bytes 73728
  32.7 0.6 %copy.19 = f32[4,32,3,3]{1,0,3,2:T(4,128)} copy(f32[4,32,3,3]{1,0,3,2:T(4,128)S(1)} %bitcast.22) | data formatting | bytes 9216
Async XLA Ops:
  0.6 0.9 %copy-start = (bf16[32,32,3,3]{1,0,3,2:T(8,128)(2,1)S(1)}, bf16[32,32,3,3]{1,0,3,2:T(8,128)(2,1)}, u32[]{:S(2)}) copy-start(bf16[32,32,3,3]{1,0,3,2:T(8,128)(2,1)} %param.14) | copy-start | bytes 55300
  1.5 0.8 %copy-start.1 = (f32[4,4,512]{2,1,0:T(4,128)S(1)}, f32[4,4,512]{2,1,0:T(4,128)}, u32[]{:S(2)}) copy-start(f32[4,4,512]{2,1,0:T(4,128)} %tr_ref.1) | copy-start | bytes 98308
  2.3 0.8 %copy-start.2 = (f32[4,4,512]{2,1,0:T(4,128)S(1)}, f32[4,4,512]{2,1,0:T(4,128)}, u32[]{:S(2)}) copy-start(f32[4,4,512]{2,1,0:T(4,128)} %fo_ref.1) | copy-start | bytes 98308
  3.0 0.8 %copy-start.3 = (f32[4,4,512]{2,1,0:T(4,128)S(1)}, f32[4,4,512]{2,1,0:T(4,128)}, u32[]{:S(2)}) copy-start(f32[4,4,512]{2,1,0:T(4,128)} %se_ref.1) | copy-start | bytes 98308
  3.8 0.7 %copy-start.4 = (bf16[80,64]{1,0:T(8,128)(2,1)S(1)}, bf16[80,64]{1,0:T(8,128)(2,1)}, u32[]{:S(2)}) copy-start(bf16[80,64]{1,0:T(8,128)(2,1)} %constant.2.clone.sp_ref) | copy-start | bytes 30724
  4.5 0.7 %copy-start.5 = (bf16[32,4,3,3]{0,1,3,2:T(4,128)(2,1)S(1)}, bf16[32,4,3,3]{0,1,3,2:T(4,128)(2,1)}, u32[]{:S(2)}) copy-start(bf16[32,4,3,3]{0,1,3,2:T(4,128)(2,1)} %param.13) | copy-start | bytes 6916
  5.2 0.7 %copy-start.6 = (bf16[4,32,3,3]{1,0,3,2:T(4,128)(2,1)S(1)}, bf16[4,32,3,3]{1,0,3,2:T(4,128)(2,1)}, u32[]{:S(2)}) copy-start(bf16[4,32,3,3]{1,0,3,2:T(4,128)(2,1)} %param.15) | copy-start | bytes 6916
  5.9 0.7 %copy-start.7 = (f32[4,512]{1,0:T(4,128)S(1)}, f32[4,512]{1,0:T(4,128)}, u32[]{:S(2)}) copy-start(f32[4,512]{1,0:T(4,128)} %ka_ref.1) | copy-start | bytes 24580
  6.6 0.7 %copy-start.8 = (s32[4,512]{1,0:T(4,128)S(1)}, s32[4,512]{1,0:T(4,128)}, u32[]{:S(2)}) copy-start(s32[4,512]{1,0:T(4,128)} %ma_ref.1) | copy-start | bytes 24580
where the time goes:
time: 33.9 us; the launch traced here: 33.4 us
  Pallas kernels  23.5 us (69%)
  local copies, waits for them, and re-layouts  9.17 us (27%)
  between operations  0.66 us (2%)
    pallas_call x1, Pallas kernels, on_device(): pl.pallas_call(functools.partial(kernel, n_lat, n_lon, halo, scale), out_...  23.5 us
    unnamed x22, local copies, waits for them, and re-layouts  9.17 us

commit v1 on v0

--- a/solution.py
+++ b/solution.py
@@ -3,13 +3,13 @@
 
 import jax
 import jax.numpy as jnp
-import numpy as np
 from jax import lax
 from jax.experimental import pallas as pl
 from jax.experimental.pallas import tpu as pltpu
 from jax.sharding import PartitionSpec as P
 
 GAIN = 0.5
+VMEM_GRANT = 63 * 1024 * 1024 + 512 * 1024
 MESH = pl.DeviceIdType.MESH
 F32 = jnp.float32
 BF16 = jnp.bfloat16
@@ -38,20 +38,19 @@
 
 
 def spread_matrix():
-    m = np.zeros((80, 64), np.float32)
-    for r in range(4):
-        for c in range(4):
-            for k in range(3):
-                m[k * 16 + r * 4 + c, k * 16 + c * 4 + r] = 1
-            m[48 + r * 4 + c, 48 + r] = 1
-            m[64 + r * 4 + c, 52 + r] = 1
-    return m
+    i = lax.broadcasted_iota(jnp.int32, (80, 64), 0)
+    k = lax.broadcasted_iota(jnp.int32, (80, 64), 1)
+    array, r, c = i // 16, (i % 16) // 4, i % 4
+    at = jnp.where(array < 3, array * 16 + c * 4 + r, 36 + array * 4 + r)
+    return (k == at).astype(F32).astype(BF16)
 
 
 def kernel(
     n_lat, n_lon, halo, scale,
-    tr_ref, fo_ref, ka_ref, ma_ref, wi_ref, wm_ref, wo_ref, se_ref, sp_ref,
-    final_ref, gin_ref, gmid_ref, gout_ref,
+    tr_hbm, fo_hbm, ka_hbm, ma_hbm, wi_hbm, wm_hbm, wo_hbm, se_hbm,
+    final_hbm, gin_hbm, gmid_hbm, gout_hbm,
+    final_ref, gin_ref, gmid_ref, gout_ref, out_sem,
+    tr_ref, fo_ref, ka_ref, ma_ref, wi_ref, wm_ref, wo_ref, se_ref, in_sem,
     pk, rbuf, st, fo, se, ka, ma, lap, sixteen,
     t_if, t_ib, t_mf, t_mb, t_of, t_ob, t_tmp, t_wide,
     src, cc, h1, h2, l2, l1, acc, chunk, rs, total, fsrc, fdst,
@@ -65,6 +64,18 @@
     blocks = GROUP + 2 * halo
     rows = 4 * blocks
     reduce_here = n_lat * n_lon == 16
+
+    loads = [
+        pltpu.make_async_copy(there, here, in_sem.at[i])
+        for i, (there, here) in enumerate(
+            (
+                (tr_hbm, tr_ref), (fo_hbm, fo_ref), (se_hbm, se_ref), (ka_hbm, ka_ref),
+                (ma_hbm, ma_ref), (wi_hbm, wi_ref), (wm_hbm, wm_ref), (wo_hbm, wo_ref),
+            )
+        )
+    ]
+    for load in loads:
+        load.start()
 
     barrier = pltpu.get_barrier_semaphore()
     if reduce_here:
@@ -83,6 +94,9 @@
             barrier, inc=1, device_id={"lat": pl_lat, "lon": pl_lon}, device_id_type=MESH
         )
 
+    spread = spread_matrix()
+    for load in loads[:5]:
+        load.wait()
     pieces = [tr_ref[c] for c in range(4)] + [fo_ref[c] for c in range(4)] + [se_ref[c] for c in range(4)]
     pieces += [ka_ref[...], ma_ref[...].astype(F32)]
     for i, piece in enumerate(pieces):
@@ -168,6 +182,8 @@
                     t_tmp[top : top + 4, r * HID : (r + 1) * HID] = parts[a * 3 + b]
         target[...] = jnp.transpose(t_tmp[0:128, 0:128])[:, 0:96].astype(BF16)
 
+    for load in loads[5:]:
+        load.wait()
     wi = [wi_ref[k].astype(F32) for k in range(9)]
     wm = [wm_ref[k].astype(F32) for k in range(9)]
     wo = [wo_ref[k].astype(F32) for k in range(9)]
@@ -207,7 +223,7 @@
             pltpu.make_async_copy(pk.at[0], rbuf.at[w, which], x_recv.at[w, which]).wait()
     for w in range(blocks):
         three = jnp.concatenate([rbuf[w, 1], rbuf[w, 0], rbuf[w, 2]], axis=1)
-        got = dot(sp_ref[...], three)
+        got = dot(spread, three)
         side = jnp.where(lane < TILE // 2, got[:, 2 * TILE :], got[:, TILE : 2 * TILE])
         both = jnp.concatenate([got[:, 0:TILE], side], axis=1)
         here = slice(w * 16, (w + 1) * 16)
@@ -386,7 +402,9 @@
         pltpu.make_async_copy(fsrc.at[0], fdst.at[i], f_recv.at[i]).wait()
     for i in range(GROUP):
         for r in range(4):
-            final_ref[r, :, i * TILE : (i + 1) * TILE] = fdst[i, r * 4 : r * 4 + 4, :]
+            final_ref[:, r, i * TILE : (i + 1) * TILE] = fdst[i, r * 4 : r * 4 + 4, :]
+    stores = [pltpu.make_async_copy(final_ref, final_hbm, out_sem.at[0])]
+    stores[0].start()
 
     if reduce_here:
         for copy in gathered:
@@ -401,12 +419,27 @@
             gmid_ref[k] = result[a * HID : (a + 1) * HID, side]
             gout_ref[k] = result[96 + a * 4 : 100 + a * 4, side]
             gin_ref[k] = result[108 + b * 4 : 112 + b * 4, a * HID : (a + 1) * HID]
-
+    for i, (here, there) in enumerate(
+        ((gin_ref, gin_hbm), (gmid_ref, gmid_hbm), (gout_ref, gout_hbm))
+    ):
+        stores.append(pltpu.make_async_copy(here, there, out_sem.at[i + 1]))
+        stores[-1].start()
     for copy, when in waits:
         if when is None:
             copy.wait_send()
         else:
             pl.when(when)(copy.wait_send)
+    for store in stores:
+        store.wait()
+
+
+def hand_on(*refs):
+    sem = refs[-1]
+    copies = [pltpu.make_async_copy(refs[i], refs[i + 4], sem.at[i]) for i in range(4)]
+    for copy in copies:
+        copy.start()
+    for copy in copies:
+        copy.wait()
 
 
 def on_device(
@@ -417,7 +450,6 @@
     blocks = GROUP + 2 * halo
     rows = 4 * blocks
     scale = 1.0 / math.sqrt(tracers.shape[1] * n_lat * tracers.shape[2] * n_lon)
-    vmem = pl.BlockSpec(memory_space=pltpu.VMEM)
     sends = 12 if halo == 0 else 36
     wi = weight_in.transpose(2, 3, 1, 0).reshape(9, 4, HID)
     wm = weight_mid.transpose(2, 3, 0, 1).reshape(9, HID, HID)
@@ -425,17 +457,30 @@
     field = pltpu.VMEM((rows * 4, WIDE), F32)
     wide = pltpu.VMEM((2, (rows + 2) * DEEP, WIDE), BF16)
     narrow = pltpu.VMEM((2, (rows + 2) * 16, WIDE), BF16)
+    hbm = pl.BlockSpec(memory_space=pltpu.HBM)
+    outs = (
+        jax.ShapeDtypeStruct((4, 4, 512), F32),
+        jax.ShapeDtypeStruct((9, 4, HID), F32),
+        jax.ShapeDtypeStruct((9, HID, HID), F32),
+        jax.ShapeDtypeStruct((9, 4, HID), F32),
+    )
     final, g_in, g_mid, g_out = pl.pallas_call(
         functools.partial(kernel, n_lat, n_lon, halo, scale),
-        out_shape=(
-            jax.ShapeDtypeStruct((4, 4, 512), F32),
-            jax.ShapeDtypeStruct((9, 4, HID), F32),
-            jax.ShapeDtypeStruct((9, HID, HID), F32),
-            jax.ShapeDtypeStruct((9, 4, HID), F32),
-        ),
-        in_specs=[vmem] * 9,
-        out_specs=(vmem,) * 4,
-        scratch_shapes=[
+        out_shape=outs,
+        in_specs=[hbm] * 8,
+        out_specs=(hbm,) * 4,
+        scratch_shapes=[pltpu.VMEM(o.shape, F32) for o in outs]
+        + [
+            pltpu.SemaphoreType.DMA((4,)),
+            pltpu.VMEM((4, 4, 512), F32),
+            pltpu.VMEM((4, 4, 512), F32),
+            pltpu.VMEM((4, 512), F32),
+            pltpu.VMEM((4, 512), jnp.int32),
+            pltpu.VMEM((9, 4, HID), BF16),
+            pltpu.VMEM((9, HID, HID), BF16),
+            pltpu.VMEM((9, 4, HID), BF16),
+            pltpu.VMEM((4, 4, 512), F32),
+            pltpu.SemaphoreType.DMA((8,)),
             pltpu.VMEM((GROUP, 64, TILE), BF16),
             pltpu.VMEM((blocks, 3, 64, TILE), BF16),
             field, field, field, field, field,
@@ -466,16 +511,21 @@
             pltpu.SemaphoreType.DMA((15,)),
         ],
         compiler_params=pltpu.CompilerParams(
-            collective_id=0, has_side_effects=True, vmem_limit_bytes=48 * 1024 * 1024
+            collective_id=0, has_side_effects=True, vmem_limit_bytes=VMEM_GRANT
         ),
-    )(
-        tracers, forcing, diffusivity, ocean_mask, wi, wm, wo, sensitivity,
-        jnp.asarray(spread_matrix(), BF16),
-    )
+    )(tracers, forcing, diffusivity, ocean_mask, wi, wm, wo, sensitivity)
     if n_lat * n_lon != 16:
         g_in, g_mid, g_out = lax.psum((g_in, g_mid, g_out), ("lon", "lat"))
+    final, g_in, g_mid, g_out = pl.pallas_call(
+        hand_on,
+        out_shape=outs,
+        in_specs=[hbm] * 4,
+        out_specs=(hbm,) * 4,
+        scratch_shapes=[pltpu.SemaphoreType.DMA((4,))],
+        compiler_params=pltpu.CompilerParams(vmem_limit_bytes=VMEM_GRANT),
+    )(final, g_in, g_mid, g_out)
     return (
-        final.transpose(1, 0, 2),
+        final,
         g_in.reshape(3, 3, 4, HID).transpose(3, 2, 0, 1),
         g_mid.reshape(3, 3, HID, HID).transpose(2, 3, 0, 1),
         g_out.reshape(3, 3, 4, HID).transpose(2, 3, 0, 1),

time: 33.9 us -> 32.8 us (0.968); the launches traced: 33.4 us -> 32.7 us
  local copies, waits for them, and re-layouts: 9.17 us -> 0 us
  Pallas kernels: 23.5 us -> 32 us
    unnamed x22 -> x0, local copies, waits for them, and re-layouts: 9.17 us -> none
    pallas_call x0 -> x1, Pallas kernels: none -> 7.72 us  [on_device(): pl.pallas_call(hand_on, out_shape=outs, in_specs=[hbm] * 4, out_specs=(hb...]
    pallas_call x1, Pallas kernels: 23.5 us -> 24.3 us  [on_device(): pl.pallas_call(functools.partial(kernel, n_lat, n_lon, halo, scale), out_...]
where the time goes in v1:
time: 32.8 us; the launch traced here: 32.7 us
  Pallas kernels  32 us (98%)
  between operations  0.64 us (2%)
    pallas_call x1, Pallas kernels, on_device(): pl.pallas_call(functools.partial(kernel, n_lat, n_lon, halo, scale), out_...  24.3 us
    pallas_call x1, Pallas kernels, on_device(): pl.pallas_call(hand_on, out_shape=outs, in_specs=[hbm] * 4, out_specs=(hb...  7.72 us

profile of v1, /device:TPU:0, one launch (start us, length us, event | category | flops | bytes accessed | tf_op | source)
XLA Modules:
  0.0 32.7 jit_solution(1158940679587185377)
XLA Ops:
  0.6 24.3 %shard_map.111 = (f32[4,4,512]{2,1,0:T(4,128)}, f32[9,4,32]{2,1,0:T(4,128)}, f32[9,32,32]{2,1,0:T(8,128)}, f32[9,4,32]{2,1,0:T(4,128)}) custom-call(f32[4,4,512]{2,1,0:T(4,128)} %tr_hbm.1, f32[4,4,512]{2,1,0:T(4,128)} %fo_hbm.1, f32[4,512]{1,0:T(4,128)} %ka_hbm.1, s32[4,512]{1,0:T(4,128)} %ma_hbm.1, bf16[9,4,32]{2,1,0:T(4,128)(2,1)} %bitcast.19, ...), custom_call_target="tpu_custom_call" | custom-call | tf_op jit(solution)/shard_map/pallas_call | solution.py:467
  24.9 7.7 %shard_map.112 = (f32[4,4,512]{2,1,0:T(4,128)}, f32[9,4,32]{2,1,0:T(4,128)}, f32[9,32,32]{2,1,0:T(8,128)}, f32[9,4,32]{2,1,0:T(4,128)}) custom-call(f32[4,4,512]{2,1,0:T(4,128)} %get-tuple-element.12.refs_0_, f32[9,4,32]{2,1,0:T(4,128)} %get-tuple-element.13.refs_1_, f32[9,32,32]{2,1,0:T(8,128)} %get-tuple-element.14.refs_2_, ...), custom_call_target="tpu_custom_call" | custom-call | tf_op jit(solution)/shard_map/pallas_call | solution.py:519

commit v2 on v1

--- a/solution.py
+++ b/solution.py
@@ -434,12 +434,16 @@
 
 
 def hand_on(*refs):
-    sem = refs[-1]
-    copies = [pltpu.make_async_copy(refs[i], refs[i + 4], sem.at[i]) for i in range(4)]
-    for copy in copies:
-        copy.start()
-    for copy in copies:
-        copy.wait()
+    there, back, held, sems = refs[:4], refs[4:8], refs[8:12], refs[12]
+    reads = [pltpu.make_async_copy(there[i], held[i], sems.at[0, i]) for i in range(4)]
+    writes = [pltpu.make_async_copy(held[i], back[i], sems.at[1, i]) for i in range(4)]
+    for read in reads:
+        read.start()
+    for read, write in zip(reads, writes):
+        read.wait()
+        write.start()
+    for write in writes:
+        write.wait()
 
 
 def on_device(
@@ -521,7 +525,8 @@
         out_shape=outs,
         in_specs=[hbm] * 4,
         out_specs=(hbm,) * 4,
-        scratch_shapes=[pltpu.SemaphoreType.DMA((4,))],
+        scratch_shapes=[pltpu.VMEM(o.shape, F32) for o in outs]
+        + [pltpu.SemaphoreType.DMA((2, 4))],
         compiler_params=pltpu.CompilerParams(vmem_limit_bytes=VMEM_GRANT),
     )(final, g_in, g_mid, g_out)
     return (

time: 32.8 us -> 26.8 us (0.82)
  Pallas kernels: 32 us -> 26 us
    pallas_call x1, Pallas kernels: 7.72 us -> 1.68 us  [on_device(): pl.pallas_call(hand_on, out_shape=outs, in_specs=[hbm] * 4, out_specs=(hb...]
where the time goes in v2:
time: 26.8 us; the launch traced here: 26.6 us
  Pallas kernels  26 us (97%)
  between operations  0.64 us (2%)
    pallas_call x1, Pallas kernels, on_device(): pl.pallas_call(functools.partial(kernel, n_lat, n_lon, halo, scale), out_...  24.3 us
    pallas_call x1, Pallas kernels, on_device(): pl.pallas_call(hand_on, out_shape=outs, in_specs=[hbm] * 4, out_specs=(hb...  1.68 us

profile of v2, /device:TPU:0, one launch (start us, length us, event | category | flops | bytes accessed | tf_op | source)
XLA Modules:
  0.0 26.6 jit_solution(249117161643639184)
XLA Ops:
  0.6 24.3 %shard_map.111 = (f32[4,4,512]{2,1,0:T(4,128)}, f32[9,4,32]{2,1,0:T(4,128)}, f32[9,32,32]{2,1,0:T(8,128)}, f32[9,4,32]{2,1,0:T(4,128)}) custom-call(f32[4,4,512]{2,1,0:T(4,128)} %tr_hbm.1, f32[4,4,512]{2,1,0:T(4,128)} %fo_hbm.1, f32[4,512]{1,0:T(4,128)} %ka_hbm.1, s32[4,512]{1,0:T(4,128)} %ma_hbm.1, bf16[9,4,32]{2,1,0:T(4,128)(2,1)} %bitcast.19, ...), custom_call_target="tpu_custom_call" | custom-call | tf_op jit(solution)/shard_map/pallas_call | solution.py:471
  24.9 1.7 %shard_map.112 = (f32[4,4,512]{2,1,0:T(4,128)}, f32[9,4,32]{2,1,0:T(4,128)}, f32[9,32,32]{2,1,0:T(8,128)}, f32[9,4,32]{2,1,0:T(4,128)}) custom-call(f32[4,4,512]{2,1,0:T(4,128)} %get-tuple-element.12.refs_0_, f32[9,4,32]{2,1,0:T(4,128)} %get-tuple-element.13.refs_1_, f32[9,32,32]{2,1,0:T(8,128)} %get-tuple-element.14.refs_2_, ...), custom_call_target="tpu_custom_call" | custom-call | tf_op jit(solution)/shard_map/pallas_call | solution.py:523

commit v3 on v2

--- a/solution.py
+++ b/solution.py
@@ -51,7 +51,7 @@
     final_hbm, gin_hbm, gmid_hbm, gout_hbm,
     final_ref, gin_ref, gmid_ref, gout_ref, out_sem,
     tr_ref, fo_ref, ka_ref, ma_ref, wi_ref, wm_ref, wo_ref, se_ref, in_sem,
-    pk, rbuf, st, fo, se, ka, ma, lap, sixteen,
+    pk, pe, rbuf, ebuf, st, fo, se, ka, ma, lap, sixteen,
     t_if, t_ib, t_mf, t_mb, t_of, t_ob, t_tmp, t_wide,
     src, cc, h1, h2, l2, l1, acc, chunk, rs, total, fsrc, fdst,
     x_send, x_recv, f_send, f_recv, rs_send, rs_recv, ag_send, ag_recv,
@@ -103,17 +103,28 @@
         t_wide[i * 4 : i * 4 + 4, :] = piece
     t_wide[56:64, :] = jnp.zeros((8, 512), F32)
     packed = t_wide[...].astype(BF16)
+    low = lax.broadcasted_iota(jnp.int32, (32, TILE), 1) < TILE // 2
     for t in range(GROUP):
         pk[t] = packed[:, t * TILE : (t + 1) * TILE]
+        upper = t_wide[0:32, t * TILE : (t + 1) * TILE]
+        lower = pltpu.roll(t_wide[32:64, t * TILE : (t + 1) * TILE], TILE // 2, 1)
+        pe[t, 0] = jnp.where(low, lower, upper).astype(BF16)
+        pe[t, 1] = jnp.where(low, upper, lower).astype(BF16)
 
     pl.semaphore_wait(barrier, len(peer_ids))
 
     waits = []
 
+    def ends(tile, slot, which):
+        if which == 1:
+            return pk.at[tile], rbuf.at[slot]
+        return pe.at[tile, which // 2], ebuf.at[slot, which // 2]
+
     def send(tile, slot, which, sem, to_lat, to_lon, when):
+        source, target = ends(tile, slot, which)
         copy = pltpu.make_async_remote_copy(
-            src_ref=pk.at[tile],
-            dst_ref=rbuf.at[slot, which],
+            src_ref=source,
+            dst_ref=target,
             send_sem=x_send.at[sem],
             recv_sem=x_recv.at[slot, which],
             device_id={"lat": to_lat, "lon": to_lon},
@@ -126,7 +137,7 @@
         waits.append((copy, when))
 
     def keep(tile, slot, which, when):
-        copy = pltpu.make_async_copy(pk.at[tile], rbuf.at[slot, which], x_recv.at[slot, which])
+        copy = pltpu.make_async_copy(*ends(tile, slot, which), x_recv.at[slot, which])
         if when is None:
             copy.start()
         else:
@@ -217,15 +228,19 @@
             return v
         return v * inside(per_row, v.shape[0], first)
 
-    lane = lax.broadcasted_iota(jnp.int32, (80, TILE), 1)
     for w in range(blocks):
         for which in range(3):
-            pltpu.make_async_copy(pk.at[0], rbuf.at[w, which], x_recv.at[w, which]).wait()
+            pltpu.make_async_copy(*ends(0, w, which), x_recv.at[w, which]).wait()
     for w in range(blocks):
-        three = jnp.concatenate([rbuf[w, 1], rbuf[w, 0], rbuf[w, 2]], axis=1)
-        got = dot(spread, three)
-        side = jnp.where(lane < TILE // 2, got[:, 2 * TILE :], got[:, TILE : 2 * TILE])
-        both = jnp.concatenate([got[:, 0:TILE], side], axis=1)
+        before, after = ebuf[w, 0].astype(F32), ebuf[w, 1].astype(F32)
+        side = jnp.concatenate(
+            [
+                jnp.where(low, after, before),
+                pltpu.roll(jnp.where(low, before, after), TILE // 2, 1),
+            ],
+            axis=0,
+        )
+        both = dot(spread, jnp.concatenate([rbuf[w], side.astype(BF16)], axis=1))
         here = slice(w * 16, (w + 1) * 16)
         st[here, :] = clear(both[0:16], 4, 4 * w)
         fo[here, :] = both[16:32]
@@ -486,7 +501,9 @@
             pltpu.VMEM((4, 4, 512), F32),
             pltpu.SemaphoreType.DMA((8,)),
             pltpu.VMEM((GROUP, 64, TILE), BF16),
-            pltpu.VMEM((blocks, 3, 64, TILE), BF16),
+            pltpu.VMEM((GROUP, 2, 32, TILE), BF16),
+            pltpu.VMEM((blocks, 64, TILE), BF16),
+            pltpu.VMEM((blocks, 2, 32, TILE), BF16),
             field, field, field, field, field,
             pltpu.VMEM((rows * 4 + 16, WIDE), F32),
             pltpu.VMEM((rows * 16, WIDE), F32),

time: 26.8 us -> 26.2 us (0.978)
  Pallas kernels: 26 us -> 25.3 us
    pallas_call x1, Pallas kernels: 24.3 us -> 23.7 us  [on_device(): pl.pallas_call(functools.partial(kernel, n_lat, n_lon, halo, scale), out_...]
where the time goes in v3:
time: 26.2 us; the launch traced here: 26 us
  Pallas kernels  25.3 us (97%)
  between operations  0.64 us (2%)
    pallas_call x1, Pallas kernels, on_device(): pl.pallas_call(functools.partial(kernel, n_lat, n_lon, halo, scale), out_...  23.7 us
    pallas_call x1, Pallas kernels, on_device(): pl.pallas_call(hand_on, out_shape=outs, in_specs=[hbm] * 4, out_specs=(hb...  1.68 us

profile of v3, /device:TPU:0, one launch (start us, length us, event | category | flops | bytes accessed | tf_op | source)
XLA Modules:
  0.0 26.0 jit_solution(8754500328449914110)
XLA Ops:
  0.6 23.7 %shard_map.111 = (f32[4,4,512]{2,1,0:T(4,128)}, f32[9,4,32]{2,1,0:T(4,128)}, f32[9,32,32]{2,1,0:T(8,128)}, f32[9,4,32]{2,1,0:T(4,128)}) custom-call(f32[4,4,512]{2,1,0:T(4,128)} %tr_hbm.1, f32[4,4,512]{2,1,0:T(4,128)} %fo_hbm.1, f32[4,512]{1,0:T(4,128)} %ka_hbm.1, s32[4,512]{1,0:T(4,128)} %ma_hbm.1, bf16[9,4,32]{2,1,0:T(4,128)(2,1)} %bitcast.19, ...), custom_call_target="tpu_custom_call" | custom-call | tf_op jit(solution)/shard_map/pallas_call | solution.py:486
  24.3 1.7 %shard_map.112 = (f32[4,4,512]{2,1,0:T(4,128)}, f32[9,4,32]{2,1,0:T(4,128)}, f32[9,32,32]{2,1,0:T(8,128)}, f32[9,4,32]{2,1,0:T(4,128)}) custom-call(f32[4,4,512]{2,1,0:T(4,128)} %get-tuple-element.12.refs_0_, f32[9,4,32]{2,1,0:T(4,128)} %get-tuple-element.13.refs_1_, f32[9,32,32]{2,1,0:T(8,128)} %get-tuple-element.14.refs_2_, ...), custom_call_target="tpu_custom_call" | custom-call | tf_op jit(solution)/shard_map/pallas_call | solution.py:540
